TPU v7x, 32 devices: a whole 2x2x4 slice. The times are simulated.
32 devices in a mesh: patch: 8 (over y, x, core), head: 4 (over z).
Axes of the slice: x: 2, y: 2, z: 4, core: 2. Of those that a mesh axis runs over, the one named last changes fastest.
Arguments:
- fresh_qkv: bfloat16 [4096, 3, 3072], P('patch', None, 'head'), may hold values from -12 to 12
- kv_cache: bfloat16 [4096, 2, 3072], P('patch', None, 'head'), may hold values from -8 to 8
- hidden: bfloat16 [4096, 3072], P('patch'), may hold values from -6 to 6
- refresh: int32 [4], replicated, may hold values from 0 to 7, as said below
- out_weight: bfloat16 [3072, 3072], P('head'), may hold values from -0.109375 to 0.109375
- final_weight: bfloat16 [3072, 64], replicated, may hold values from -0.109375 to 0.109375
- final_bias: float32 [64], replicated, may hold values from -3 to 3
- gate_scale: float32 [3072], replicated, may hold values from 0.1 to 1.9
- noise_level: float32 [1], replicated, may hold values from 0.15 to 0.35
- noisy_latent: bfloat16 [16, 16, 1024], P('patch'), may hold values from -6 to 6
- velocity_cache: bfloat16 [16, 16, 1024], P('patch'), may hold values from -6 to 6
- conv_weight: bfloat16 [512, 3, 3, 16], P('head'), may hold values from -0.5 to 0.5
- conv_bias: float32 [512], P('head'), may hold values from -3 to 3
Outputs:
- decoded: bfloat16 [16, 512, 1024], P('patch', 'head')
Inputs may be any that keep to these rules, and one draw needn't show every extreme that they name: 4 distinct patch indices; refresh[1] is 7.
All inputs are finite; a program needn't handle non-finite values.
Results may differ from a plain program's by a relative error of at most 0.0044.
The roundings to bfloat16 on the way count: a program that leaves them out, or rounds other values in their place, can miss the bound.
Values may be sent and summed in bfloat16 or wider, within the bound.
A program may use at most 128 MiB of HBM per device.

v0:
```python
import math

import jax
import jax.numpy as jnp
from jax import lax
from jax.sharding import PartitionSpec as P

HEAD_DIM = 128
LAT_CH = 16
GW = 512
ROWS_DEV = 1
REFRESH = 4
TOK_DEV = 512


def broadcast(block, axis, source):
    block = jnp.where(lax.axis_index(axis) == source, block, jnp.zeros_like(block))
    return lax.psum(block, axis)


def padded_2(cells, sides, width):
    for axis, dim in sides:
        count = lax.axis_size(axis)
        ends = count - 1
        head = lax.slice_in_dim(cells, 0, width, axis=dim)
        tail = lax.slice_in_dim(cells, cells.shape[dim] - width, cells.shape[dim], axis=dim)
        cells = jnp.concatenate(
            [
                lax.ppermute(tail, axis, [(i, (i + 1) % count) for i in range(ends)]),
                cells,
                lax.ppermute(head, axis, [((i + 1) % count, i) for i in range(ends)]),
            ],
            axis=dim,
        )
    return cells


def on_device(
    fresh_qkv,
    kv_cache,
    hidden,
    refresh,
    out_weight,
    final_weight,
    final_bias,
    gate_scale,
    noise_level,
    noisy_latent,
    velocity_cache,
    conv_weight,
    conv_bias,
):
    own_index = lax.axis_index("patch")
    selector = (refresh == own_index).astype(jnp.float32)
    refreshed = jnp.sum(selector) > 0.5
    key_rows = jnp.where(refreshed, fresh_qkv[:, 1], kv_cache[:, 0])
    value_rows = jnp.where(refreshed, fresh_qkv[:, 2], kv_cache[:, 1])
    local_width = fresh_qkv.shape[2]
    heads_here = local_width // HEAD_DIM
    pieces = []
    for refresh_slot in range(REFRESH):
        pieces.append(broadcast(fresh_qkv[:, 0], "patch", refresh[refresh_slot]))
    queries = jnp.concatenate(pieces, axis=0)
    total_rows = queries.shape[0]
    block_rows = math.gcd(total_rows, 512)
    blocks = total_rows // block_rows
    query_blocks = queries.reshape(blocks, block_rows, heads_here, HEAD_DIM)
    key_heads = key_rows.reshape(-1, heads_here, HEAD_DIM)
    value_heads = value_rows.reshape(-1, heads_here, HEAD_DIM)
    score_scale = 1.0 / math.sqrt(HEAD_DIM)

    def block_scores(query_block):
        scores = (
            jnp.einsum("qhd,khd->hqk", query_block, key_heads, preferred_element_type=jnp.float32)
            * score_scale
        )
        return (scores, jnp.max(scores, axis=2))

    all_scores, maxima = lax.map(block_scores, query_blocks)
    maxima = lax.pmax(maxima, "patch")

    def block_sums(inputs):
        scores, block_max = inputs
        exp_scores = jnp.exp(scores - block_max[:, :, None])
        denominator = jnp.sum(exp_scores, axis=2)
        numerator = jnp.einsum(
            "hqk,khd->qhd",
            exp_scores.astype(jnp.bfloat16),
            value_heads,
            preferred_element_type=jnp.float32,
        )
        return (numerator, denominator)

    numerator, denominator = lax.map(block_sums, (all_scores, maxima))
    numerator = numerator.reshape(total_rows, heads_here, HEAD_DIM)
    denominator = jnp.transpose(denominator, (0, 2, 1)).reshape(total_rows, heads_here)
    final_wide = final_weight.astype(jnp.float32)
    gated_final = gate_scale[:, None] * final_wide
    operand = numerator.reshape(total_rows, local_width)
    summed, shared_denominator = (
        lax.psum_scatter(operand, "patch", scatter_dimension=0, tiled=True),
        lax.psum_scatter(denominator, "patch", scatter_dimension=0, tiled=True),
    )
    rows_here = summed.shape[0]
    attention = summed / jnp.repeat(shared_denominator, HEAD_DIM, axis=1)
    projected = jnp.dot(attention, out_weight.astype(jnp.float32), precision=lax.Precision.HIGH)
    velocity_part = jnp.dot(projected, gated_final, precision=lax.Precision.HIGH)
    gathered = lax.all_gather(velocity_part, ("patch", "head"), axis=0, tiled=True)
    gathered = gathered.reshape(lax.axis_size("patch"), lax.axis_size("head"), rows_here, -1).sum(
        axis=1
    )
    gathered = gathered.reshape(REFRESH, TOK_DEV, -1)
    attention_term = jnp.sum(selector[:, None, None] * gathered, axis=0)
    velocity_fresh = jnp.dot(hidden, final_weight, preferred_element_type=jnp.float32) + final_bias
    velocity_fresh = velocity_fresh + attention_term
    fresh_field = velocity_fresh.reshape(ROWS_DEV, GW, LAT_CH, 2, 2)
    fresh_field = jnp.transpose(fresh_field, (0, 3, 2, 1, 4)).reshape(2 * ROWS_DEV, LAT_CH, 2 * GW)
    velocity_field = jnp.where(refreshed, fresh_field, velocity_cache.astype(jnp.float32))
    latent = noisy_latent.astype(jnp.float32) - noise_level[0] * velocity_field
    decoder_in = (latent / 0.3611 + 0.1159).astype(jnp.bfloat16)
    padded = padded_2(decoder_in, (("patch", 0),), 1)
    padded = jnp.pad(padded, ((0, 0), (0, 0), (1, 1)))
    row_count = decoder_in.shape[0]
    columns = decoder_in.shape[2]
    stencil = jnp.stack(
        [
            padded[row_shift : row_shift + row_count, :, col_shift : col_shift + columns]
            for row_shift in range(3)
            for col_shift in range(3)
        ],
        axis=1,
    )
    stencil = stencil.reshape(row_count, -1, columns)
    kernel = conv_weight.reshape(conv_weight.shape[0], -1)
    decoded = jnp.einsum("oc,rcw->row", kernel, stencil, preferred_element_type=jnp.float32)
    decoded = decoded + conv_bias[None, :, None]
    return decoded.astype(jnp.bfloat16)


def solution(mesh):
    return jax.shard_map(
        on_device,
        mesh=mesh,
        in_specs=(
            P("patch", None, "head"),
            P("patch", None, "head"),
            P("patch", None),
            P(),
            P("head", None),
            P(),
            P(),
            P(),
            P(),
            P("patch", None, None),
            P("patch", None, None),
            P("head", None, None, None),
            P("head"),
        ),
        out_specs=P("patch", "head", None),
        check_vma=False,
    )
```

profile of v0, /device:TPU:0, one launch (start us, length us, event | category | flops | bytes accessed | tf_op | source)
XLA Modules:
  0.0 579.4 jit_solution(7649955441296965320)
XLA Ops:
  10.5 3.9 fusion.37
  16.8 2.3 copy.94
  19.1 5.9 %fusion.38 = (bf16[512,1,768]{2,1,0:T(2,128)(2,1)}, bf16[512,1,768]{2,1,0:T(2,128)(2,1)}) fusion(bf16[512,2,768]{2,1,0:T(2,128)(2,1)} %param.18), kind=kLoop, calls=%fused_computation.66 | loop fusion | bytes 3145728 | tf_op jit(solution)/shard_map/slice | solution.py:57
  25.0 4.7 copy.93
  29.7 4.7 copy.95
  35.5 2.7 broadcast_select_fusion
  42.8 44.5 %all-reduce.4.cloned.1.call-done = (bf16[512,768]{1,0:T(8,128)(2,1)}, bf16[512,768]{1,0:T(8,128)(2,1)}, bf16[512,768]{1,0:T(8,128)(2,1)}, bf16[512,768]{1,0:T(8,128)(2,1)}) async-done(((bf16[512,768]{1,0:T(8,128)(2,1)}, bf16[512,768]{1,0:T(8,128)(2,1)}, bf16[512,768]{1,0:T(8,128)(2,1)}, bf16[512,768]{1,0:T(8,128)(2,1)}), (bf16[512,768]{1,0:T(8,128)(2,1)}, bf16[512,768]{1,0:T(8,128)(2,1)}, ...) | async-done | bytes 3145744 | tf_op jit(solution)/shard_map/psum | solution.py:18
  87.3 3.3 pad_maximum_fusion
  90.6 7.7 %reshape.65 = bf16[4,512,6,128]{3,2,1,0:T(8,128)(2,1)} reshape(bf16[2048,768]{1,0:T(8,128)(2,1)} %pad_maximum_fusion) | data formatting | bytes 6291456 | tf_op jit(solution)/shard_map/reshape | solution.py:67
  98.2 4.5 copy.68
  102.8 23.4 %while.24 = (s32[]{:T(128)}, f32[4,6,512,512]{2,3,1,0:T(8,128)}, f32[4,6,512]{2,1,0:T(8,128)S(1)}, bf16[4,512,6,128]{3,1,2,0:T(8,128)(2,1)}, bf16[512,6,128]{2,0,1:T(8,128)(2,1)}, /*index=5*/s32[]{:T(128)}) while((s32[]{:T(128)}, f32[4,6,512,512]{2,3,1,0:T(8,128)}, f32[4,6,512]{2,1,0:T(8,128)S(1)}, bf16[4,512,6,128]{3,1,2,0:T(8,128)(2,1)}, ...), condition=%wide.region_7.8_spmd, body=%wide.region_5.7_spmd.sunk | while | flops 407368704 | bytes 20493384 | solution.py:79
  102.8 5.0 bitcast_dynamic-update-slice_fusion.7
  108.6 4.9 bitcast_dynamic-update-slice_fusion.7
  114.4 5.0 bitcast_dynamic-update-slice_fusion.7
  120.3 5.1 bitcast_dynamic-update-slice_fusion.7
  126.2 23.7 %pmax.7 = f32[4,6,512]{2,1,0:T(8,128)S(1)} all-reduce(f32[4,6,512]{2,1,0:T(8,128)S(1)} %get-tuple-element.67), channel_id=1, replica_groups=mesh['patch'=8,'head'=4] {'patch'}, use_global_device_ids=true, to_apply=%region_8.9 | all-reduce | flops 12288 | bytes 98304 | tf_op jit(solution)/shard_map/pmax | solution.py:80
  149.9 233.3 %while.25 = (s32[]{:T(128)}, f32[4,512,6,128]{1,0,3,2:T(4,128)}, f32[4,6,512]{2,1,0:T(8,128)S(1)}, f32[4,6,512,512]{2,3,1,0:T(8,128)}, f32[4,6,512]{2,1,0:T(8,12...) while((s32[]{:T(128)}, f32[4,512,6,128]{1,0,3,2:T(4,128)}, f32[4,6,512]{2,1,0:T(8,128)S(1)}, ...), condition=%wide.region_11.12_spmd, body=%wide.region_9.11_spmd.sunk | while | flops 408941568 | bytes 46493796 | solution.py:94
  149.9 6.8 %constant_dynamic-slice_fusion.2 = f32[1,6,512,512]{2,3,1,0:T(8,128)} fusion(f32[4,6,512,512]{2,3,1,0:T(8,128)} %get-tuple-element.264, s32[]{:T(128)} %get-tuple-element.253), kind=kLoop, calls=%fused_computation.16.clone.1 | loop fusion | bytes 12582916 | tf_op jit(solution)/shard_map/while/body/jit(dynamic_index_in_dim)/dynamic_slice | solution.py:94
  156.7 6.7 %copy.102 = f32[1,6,512,512]{3,2,1,0:T(8,128)} copy(f32[1,6,512,512]{2,3,1,0:T(8,128)} %constant_dynamic-slice_fusion.2) | data formatting | bytes 12582912 | tf_op jit(solution)/shard_map/while/body/jit(dynamic_index_in_dim)/dynamic_slice | solution.py:94
  163.4 5.4 fusion.59
  168.8 4.8 copy.103
  173.6 31.0 %dynamic_update_slice.25 = f32[4,512,6,128]{1,0,3,2:T(4,128)} dynamic-update-slice(f32[4,512,6,128]{1,0,3,2:T(4,128)} %get-tuple-element.254, f32[1,512,6,128]{1,0,3,2:T(1,128)} %copy.103, s32[]{:T(128)} %get-tuple-element.253, s32[]{:T(128)} %constant.48.clone.1..sunk, s32[]{:T(128)} %constant.48.clone.1..sunk, s32[]{:T(128)} %constant.48.clone.1..sunk) | dynamic-update-slice | bytes 3145732 | tf_op jit(solution)/shard_map/while/body/jit(dynamic_update_index_in_dim)/dynamic_update_slice | solution.py:94
  204.7 3.6 fusion.60
  208.3 6.8 %constant_dynamic-slice_fusion.2 = f32[1,6,512,512]{2,3,1,0:T(8,128)} fusion(f32[4,6,512,512]{2,3,1,0:T(8,128)} %get-tuple-element.264, s32[]{:T(128)} %get-tuple-element.253), kind=kLoop, calls=%fused_computation.16.clone.1 | loop fusion | bytes 12582916 | tf_op jit(solution)/shard_map/while/body/jit(dynamic_index_in_dim)/dynamic_slice | solution.py:94
  215.1 6.7 %copy.102 = f32[1,6,512,512]{3,2,1,0:T(8,128)} copy(f32[1,6,512,512]{2,3,1,0:T(8,128)} %constant_dynamic-slice_fusion.2) | data formatting | bytes 12582912 | tf_op jit(solution)/shard_map/while/body/jit(dynamic_index_in_dim)/dynamic_slice | solution.py:94
  221.7 5.4 fusion.59
  227.1 4.8 copy.103
  231.9 31.0 %dynamic_update_slice.25 = f32[4,512,6,128]{1,0,3,2:T(4,128)} dynamic-update-slice(f32[4,512,6,128]{1,0,3,2:T(4,128)} %get-tuple-element.254, f32[1,512,6,128]{1,0,3,2:T(1,128)} %copy.103, s32[]{:T(128)} %get-tuple-element.253, s32[]{:T(128)} %constant.48.clone.1..sunk, s32[]{:T(128)} %constant.48.clone.1..sunk, s32[]{:T(128)} %constant.48.clone.1..sunk) | dynamic-update-slice | bytes 3145732 | tf_op jit(solution)/shard_map/while/body/jit(dynamic_update_index_in_dim)/dynamic_update_slice | solution.py:94
  263.0 3.6 fusion.60
  266.6 6.8 %constant_dynamic-slice_fusion.2 = f32[1,6,512,512]{2,3,1,0:T(8,128)} fusion(f32[4,6,512,512]{2,3,1,0:T(8,128)} %get-tuple-element.264, s32[]{:T(128)} %get-tuple-element.253), kind=kLoop, calls=%fused_computation.16.clone.1 | loop fusion | bytes 12582916 | tf_op jit(solution)/shard_map/while/body/jit(dynamic_index_in_dim)/dynamic_slice | solution.py:94
  273.4 6.7 %copy.102 = f32[1,6,512,512]{3,2,1,0:T(8,128)} copy(f32[1,6,512,512]{2,3,1,0:T(8,128)} %constant_dynamic-slice_fusion.2) | data formatting | bytes 12582912 | tf_op jit(solution)/shard_map/while/body/jit(dynamic_index_in_dim)/dynamic_slice | solution.py:94
  280.1 5.4 fusion.59
  285.4 4.8 copy.103
  290.3 31.0 %dynamic_update_slice.25 = f32[4,512,6,128]{1,0,3,2:T(4,128)} dynamic-update-slice(f32[4,512,6,128]{1,0,3,2:T(4,128)} %get-tuple-element.254, f32[1,512,6,128]{1,0,3,2:T(1,128)} %copy.103, s32[]{:T(128)} %get-tuple-element.253, s32[]{:T(128)} %constant.48.clone.1..sunk, s32[]{:T(128)} %constant.48.clone.1..sunk, s32[]{:T(128)} %constant.48.clone.1..sunk) | dynamic-update-slice | bytes 3145732 | tf_op jit(solution)/shard_map/while/body/jit(dynamic_update_index_in_dim)/dynamic_update_slice | solution.py:94
  321.3 3.6 fusion.60
  324.9 6.8 %constant_dynamic-slice_fusion.2 = f32[1,6,512,512]{2,3,1,0:T(8,128)} fusion(f32[4,6,512,512]{2,3,1,0:T(8,128)} %get-tuple-element.264, s32[]{:T(128)} %get-tuple-element.253), kind=kLoop, calls=%fused_computation.16.clone.1 | loop fusion | bytes 12582916 | tf_op jit(solution)/shard_map/while/body/jit(dynamic_index_in_dim)/dynamic_slice | solution.py:94
  331.7 6.7 %copy.102 = f32[1,6,512,512]{3,2,1,0:T(8,128)} copy(f32[1,6,512,512]{2,3,1,0:T(8,128)} %constant_dynamic-slice_fusion.2) | data formatting | bytes 12582912 | tf_op jit(solution)/shard_map/while/body/jit(dynamic_index_in_dim)/dynamic_slice | solution.py:94
  338.4 5.4 fusion.59
  343.8 4.8 copy.103
  348.6 31.0 %dynamic_update_slice.25 = f32[4,512,6,128]{1,0,3,2:T(4,128)} dynamic-update-slice(f32[4,512,6,128]{1,0,3,2:T(4,128)} %get-tuple-element.254, f32[1,512,6,128]{1,0,3,2:T(1,128)} %copy.103, s32[]{:T(128)} %get-tuple-element.253, s32[]{:T(128)} %constant.48.clone.1..sunk, s32[]{:T(128)} %constant.48.clone.1..sunk, s32[]{:T(128)} %constant.48.clone.1..sunk) | dynamic-update-slice | bytes 3145732 | tf_op jit(solution)/shard_map/while/body/jit(dynamic_update_index_in_dim)/dynamic_update_slice | solution.py:94
  379.6 3.6 fusion.60
  384.1 8.5 %copy.99 = f32[96,8,4,512]{3,1,2,0:T(8,128)} copy(f32[96,8,4,512]{3,2,1,0:T(4,128)} %bitcast.151) | data formatting | bytes 12582912
  392.6 24.2 %reduce-scatter.5.cloned.1.call-done = f32[256,6]{0,1:T(8,128)} async-done(((f32[2048,6]{0,1:T(8,128)}), f32[256,6]{0,1:T(8,128)}) %reduce-scatter.5.cloned.1.call-update) | async-done | bytes 6160 | tf_op jit(solution)/shard_map/reduce_scatter | solution.py:102
  416.8 65.2 %reduce-scatter.3.cloned.1.call-done = f32[256,768]{0,1:T(8,128)} async-done(((f32[2048,768]{0,1:T(8,128)}), f32[256,768]{0,1:T(8,128)}) %reduce-scatter.3.cloned.1.call-update) | async-done | bytes 786448 | tf_op jit(solution)/shard_map/reduce_scatter | solution.py:101
  483.2 4.6 fusion.41
  490.8 54.5 %all-gather.2.cloned.1.call-done = f32[8192,64]{0,1:T(8,128)} async-done(((f32[256,64]{0,1:T(8,128)}), f32[8192,64]{0,1:T(8,128)}) %all-gather.2.cloned.1.call-update) | async-done | bytes 2097168 | tf_op jit(solution)/shard_map/all_gather | solution.py:108
  545.3 3.6 reshape.58
  548.9 3.7 reduce_sum.37
  (73 shorter events, 37.0 us)
Async XLA Ops:
  6.5 549.6 %copy-start = (bf16[512,3072]{1,0:T(8,128)(2,1)S(1)}, bf16[512,3072]{1,0:T(8,128)(2,1)}, u32[]{:S(2)}) copy-start(bf16[512,3072]{1,0:T(8,128)(2,1)} %param.19) | copy-start | bytes 9437188
  6.5 80.7 %all-reduce.4.cloned.1.call-start = ((), (), s32[]{:S(2)}) async-start(), calls=%async_computation.5 | async-start | bytes 6291456 | tf_op jit(solution)/shard_map/psum | solution.py:18
  14.4 402.4 %reduce-scatter.5.cloned.1.call-start = ((), (), s32[]{:S(2)}) async-start(), calls=%async_computation.3 | async-start | bytes 73728 | tf_op jit(solution)/shard_map/reduce_scatter | solution.py:102
  16.8 17.6 %copy-start.3 = (s32[4]{0:T(128)S(1)}, s32[4]{0:T(128)}, u32[]{:S(2)}) copy-start(s32[4]{0:T(128)} %param.20) | copy-start | bytes 52
  383.2 0.6 copy-start.2
  383.9 98.1 %reduce-scatter.3.cloned.1.call-start = ((), (), s32[]{:S(2)}) async-start(), calls=%async_computation.2 | async-start | bytes 7077888 | tf_op jit(solution)/shard_map/reduce_scatter | solution.py:101
  392.6 152.7 %all-gather.2.cloned.1.call-start = ((), (), s32[]{:S(2)}) async-start(), calls=%async_computation.4 | async-start | bytes 2162688 | tf_op jit(solution)/shard_map/all_gather | solution.py:108
  483.2 4.7 copy-start.1
  483.2 4.7 copy-start.4
  487.9 68.3 %copy-start.5 = (f32[64]{0:T(128)S(1)}, f32[64]{0:T(128)}, u32[]{:S(2)}) copy-start(f32[64]{0:T(128)} %param.23) | copy-start | bytes 772
  552.6 16.2 %copy-start.6 = (f32[128]{0:T(128)S(1)}, f32[128]{0:T(128)}, u32[]{:S(2)}) copy-start(f32[128]{0:T(128)} %param.29) | copy-start | bytes 1540
  562.6 3.5 collective-permute-start
  564.8 3.5 collective-permute-start.1
Sparse Core Ops, SparseCore 0:
  14.5 72.7 all-reduce.3
  384.0 32.7 reduce-scatter.4
  420.2 61.7 reduce-scatter.2
  490.2 54.9 all-gather.1
where the time goes:
time: 587 us; the launch traced here: 579 us
  local copies, waits for them, and re-layouts  257 us (44%)
  waiting for transfers between devices  191 us (33%)
  matrix products  52.1 us (9%)
  other arithmetic  35.4 us (6%)
  blocking collectives  23.7 us (4%)
  between operations  17.1 us (3%)
    dynamic_update_slice x8, local copies, waits for them, and re-layouts, on_device(): numerator, denominator = lax.map(block_sums, (all_scores, maxima))  143 us
    reduce_scatter x1, waiting for transfers between devices, on_device(): lax.psum_scatter(operand, 'patch', scatter_dimension=0, tiled=True)  65.2 us
    all_gather x1, waiting for transfers between devices, on_device(): lax.all_gather(velocity_part, ('patch', 'head'), axis=0, tiled=True)  54.5 us
    dynamic_slice x8, local copies, waits for them, and re-layouts, on_device(): numerator, denominator = lax.map(block_sums, (all_scores, maxima))  54 us
    psum x1, waiting for transfers between devices, broadcast(): return lax.psum(block, axis)  44.5 us
    reduce_scatter x1, waiting for transfers between devices, on_device(): lax.psum_scatter(denominator, 'patch', scatter_dimension=0, tiled=True)  24.2 us
    pmax x1, blocking collectives, on_device(): maxima = lax.pmax(maxima, 'patch')  23.7 us
    unnamed x25, local copies, waits for them, and re-layouts  23.3 us
  transfers between devices with their start and end apart: 6, of which 5 were waited for; matrix products, arithmetic and copies ran while one was open for 6% of the time, Pallas kernels for 0%

commit v1 on v0

v1 whole, which is shorter than its diff:
```python
import functools
import math

import jax
import jax.numpy as jnp
from jax import lax
from jax.experimental import pallas as pl
from jax.experimental.pallas import tpu as pltpu
from jax.sharding import PartitionSpec as P

HEAD_DIM = 128
LAT_CH = 16
REFRESH = 4
MESH = pl.DeviceIdType.MESH
SCALE2 = math.log2(math.e) / math.sqrt(HEAD_DIM)
NT = (((1,), (1,)), ((), ()))
TN = (((0,), (0,)), ((), ()))
F32 = jnp.float32
BF16 = jnp.bfloat16


def iota(shape, dim):
    return lax.broadcasted_iota(jnp.int32, shape, dim)


def q_slots(n, heads):
    return heads if n == 8 else min(2, heads)


def to_column(row):
    size = row.shape[1]
    eye = iota((size, size), 0) == iota((size, size), 1)
    return jnp.sum(jnp.where(eye, row, 0.0), axis=1, keepdims=True)


def kernel(
    n,
    nz,
    heads,
    tok,
    refresh,
    noise,
    fresh,
    kv,
    hidden,
    out_weight,
    final_t,
    bias,
    gate,
    noisy,
    cache,
    conv_t,
    conv_bias,
    out,
    *scratch,
):
    slots = q_slots(n, heads)
    q_all = [scratch[h % slots] for h in range(heads)]
    stats = scratch[slots : slots + heads]
    (
        fresh_kv,
        hidden_v,
        weight_v,
        keys,
        values_t,
        w2,
        u_buf,
        spread,
        hid_t,
        rs_out,
        rs_in,
        z_buf,
        ag,
        dec,
        halo,
        load_sem,
        own_sem,
        q_send,
        q_recv,
        st_send,
        st_recv,
        rs_send,
        rs_recv,
        z_send,
        z_recv,
        ag_send,
        ag_recv,
        halo_send,
        halo_recv,
        free_sem,
    ) = scratch[slots + heads :]
    me = lax.axis_index("patch")
    mz = lax.axis_index("head")
    vec = final_t.shape[0]
    rows = vec // n

    def peers(count, body):
        if count <= 8:
            for step in range(1, count):
                body(step)
        else:
            pl.loop(1, count)(body)

    def other(step):
        return lax.rem(me + step, n)

    def other_z(step):
        return lax.rem(mz + step, nz)

    def remote(src, dst, send, recv, **where):
        return pltpu.make_async_remote_copy(
            src_ref=src,
            dst_ref=dst,
            send_sem=send,
            recv_sem=recv,
            device_id=where,
            device_id_type=MESH,
        )

    loads = [
        pltpu.make_async_copy(fresh.at[1], fresh_kv.at[0], load_sem.at[0]),
        pltpu.make_async_copy(fresh.at[2], fresh_kv.at[1], load_sem.at[1]),
        pltpu.make_async_copy(out_weight, weight_v, load_sem.at[2]),
        pltpu.make_async_copy(hidden, hidden_v, load_sem.at[3]),
    ]
    own_q = [fresh.at[0, :, pl.ds(h * HEAD_DIM, HEAD_DIM)] for h in range(heads)]
    own_copies = [
        pltpu.make_async_copy(own_q[h], q_all[h].at[me], own_sem.at[h]) for h in range(heads)
    ]
    for copy in loads + own_copies[:slots]:
        copy.start()

    barrier = pltpu.get_barrier_semaphore()
    peers(n, lambda d: pl.semaphore_signal(
        barrier, inc=1, device_id={"patch": other(d)}, device_id_type=MESH))
    peers(nz, lambda d: pl.semaphore_signal(
        barrier, inc=1, device_id={"head": other_z(d)}, device_id_type=MESH))
    pl.semaphore_wait(barrier, n - 1 + nz - 1)

    if n == 8:
        near = me + 1 - 2 * lax.rem(me, 2)
        side = me + 2 - 4 * lax.rem(me // 2, 2)
        over = me + 4 - 8 * (me // 4)
        diag = side + over - me
        half = tok // 2
        low, high = pl.ds(0, half), pl.ds(half, half)
        near_of = lambda p: p + near - me

        def q_copy(h, kind, src, dst, to):
            return remote(src, dst, q_send.at[h, kind], q_recv.at[h, kind], patch=to)

        def first(h):
            dst = q_all[h].at[me]
            return [q_copy(h, k, own_q[h], dst, to) for k, to in ((0, side), (1, over), (2, near))]

        def second(h):
            from_side, from_over = q_all[h].at[side], q_all[h].at[over]
            return [
                q_copy(h, 3, from_side.at[low], from_side.at[low], over),
                q_copy(h, 4, from_over.at[high], from_over.at[high], side),
                q_copy(h, 5, from_side, from_side, near),
                q_copy(h, 6, from_over, from_over, near),
            ]

        def third(h):
            block = q_all[h].at[diag]
            return [q_copy(h, 7, block, block, near)]

        def arrive(h, kind, dst):
            q_copy(h, kind, dst, dst, near).wait_recv()

        def start(copies):
            for copy in copies:
                copy.start()

        def relay(h):
            arrive(h, 0, q_all[h].at[side])
            arrive(h, 1, q_all[h].at[over])
            start(second(h))

        def relay_last(h):
            arrive(h, 3, q_all[h].at[diag].at[low])
            arrive(h, 4, q_all[h].at[diag].at[high])
            start(third(h))

        def before(h):
            if h + 2 < heads:
                start(first(h + 2))
            if h + 1 < heads:
                relay(h + 1)
            relay_last(h)
            arrive(h, 2, q_all[h].at[near])
            arrive(h, 5, q_all[h].at[near_of(side)])
            arrive(h, 6, q_all[h].at[near_of(over)])
            arrive(h, 7, q_all[h].at[near_of(diag)])

        def prologue():
            for h in range(min(2, heads)):
                start(first(h))

        def middle():
            relay(0)

        def refill(h):
            pass

        def sent():
            for h in range(heads):
                for copy in first(h) + second(h) + third(h):
                    copy.wait_send()

    else:

        def direct(h, d):
            return remote(
                own_q[h], q_all[h].at[me], q_send.at[h, d], q_recv.at[h, d], patch=other(d)
            )

        def prologue():
            for h in range(slots):
                peers(n, lambda d: direct(h, d).start())

        def refill(h):
            later = h + slots
            if later < heads:
                peers(n, lambda d: pl.semaphore_signal(
                    free_sem.at[h], inc=1, device_id={"patch": other(d)}, device_id_type=MESH))
                pl.semaphore_wait(free_sem.at[h], n - 1)
                own_copies[later].start()
                peers(n, lambda d: direct(later, d).start())

        def middle():
            pass

        def before(h):
            peers(n, lambda d: direct(h, d).wait_recv())

        def sent():
            for h in range(heads):
                peers(n, lambda d: direct(h, d).wait_send())

    prologue()

    is_mine = [refresh[s] == me for s in range(REFRESH)]
    mine = is_mine[0] | is_mine[1] | is_mine[2] | is_mine[3]
    group = 128
    r, c = iota((2 * group, 2 * group), 0), iota((2 * group, 2 * group), 1)
    unmix = (c == jnp.where(r < group, 2 * r, 2 * (r - group) + 1)).astype(BF16)
    eye = (iota((HEAD_DIM, HEAD_DIM), 0) == iota((HEAD_DIM, HEAD_DIM), 1)).astype(BF16)
    loads[0].wait()
    loads[1].wait()
    for g in range(tok // group):
        at = pl.ds(g * group, group)
        mixed = jnp.dot(unmix, kv[pl.ds(2 * g * group, 2 * group), :], preferred_element_type=F32)
        mixed = mixed.astype(BF16)
        keys[at, :] = jnp.where(mine, fresh_kv[0, at, :], mixed[:group])
        picked = jnp.where(mine, fresh_kv[1, at, :], mixed[group:])
        for h in range(heads):
            cols = slice(h * HEAD_DIM, (h + 1) * HEAD_DIM)
            values_t[h, :, at] = lax.dot_general(
                eye, picked[:, cols], NT, preferred_element_type=F32
            ).astype(BF16)
    middle()

    k_of = iota((vec, vec), 1)
    r_of = iota((vec, vec), 0)
    row_k = (r_of & (LAT_CH - 1)) * 4 + (r_of >> 5) * 2 + ((r_of >> 4) & 1)
    order = k_of == row_k
    final_rows = jnp.dot(order.astype(BF16), final_t[...], preferred_element_type=F32)
    gated = final_rows * gate[...]
    gated_hi = gated.astype(BF16)
    gated_lo = (gated - gated_hi.astype(F32)).astype(BF16)
    loads[2].wait()
    w2_f = lax.dot_general(
        jnp.concatenate([gated_hi, gated_lo], axis=0), weight_v[...], NT, preferred_element_type=F32
    )
    w2_f = w2_f[:vec] + w2_f[vec:]
    w2_hi = w2_f.astype(BF16)
    w2[:vec, :] = w2_hi
    w2[vec:, :] = (w2_f - w2_hi.astype(F32)).astype(BF16)
    loads[3].wait()
    bias_col = jnp.sum(jnp.where(order, bias[...], 0.0), axis=1, keepdims=True)
    hid_t[...] = bias_col + lax.dot_general(
        final_rows.astype(BF16), hidden_v[...], NT, preferred_element_type=F32
    )
    rr, cc = iota(spread.shape, 0), iota(spread.shape, 1)
    spread[...] = (cc == jnp.where(rr < tok, 2 * rr, 2 * (rr - tok) + 1)).astype(BF16)

    def st_copy(h, d):
        part = stats[h].at[me]
        return remote(part, part, st_send.at[h, d], st_recv.at[h, d], patch=other(d))

    for h in range(heads):
        own_copies[h].wait()
        before(h)
        cols = slice(h * HEAD_DIM, (h + 1) * HEAD_DIM)

        @pl.loop(0, REFRESH)
        def _(s):
            query = q_all[h][refresh[s]]
            scores = lax.dot_general(keys[:, cols], query, NT, preferred_element_type=F32)
            top = jnp.max(scores, axis=0, keepdims=True)
            weights = jnp.exp2((scores - top) * SCALE2)
            stats[h][me, pl.ds(s, 1), :] = top
            stats[h][me, pl.ds(s + REFRESH, 1), :] = jnp.sum(weights, axis=0, keepdims=True)
            num = jnp.dot(values_t[h], weights.astype(BF16), preferred_element_type=F32)
            num_hi = num.astype(BF16)
            num_lo = (num - num_hi.astype(F32)).astype(BF16)
            both = jnp.dot(w2[:, cols], num_hi, preferred_element_type=F32)
            rest = jnp.dot(w2[:vec, cols], num_lo, preferred_element_type=F32)
            u_buf[h, s] = both[:vec] + both[vec:] + rest

        peers(n, lambda d: st_copy(h, d).start())
        refill(h)

    sums = [jnp.zeros((vec, tok), F32) for _ in range(REFRESH)]
    for h in range(heads):
        peers(n, lambda d: st_copy(h, d).wait_recv())
        every = stats[h][...]
        tops, dens = every[:, :REFRESH], every[:, REFRESH:]
        top = jnp.max(tops, axis=0)
        den = jnp.sum(dens * jnp.exp2((tops - top[None]) * SCALE2), axis=0)
        factor = jnp.exp2((stats[h][me][:REFRESH] - top) * SCALE2) / den
        for s in range(REFRESH):
            sums[s] = sums[s] + u_buf[h, s] * factor[s : s + 1]
    for p in range(n):
        for s in range(REFRESH):
            rs_out[p, s] = sums[s][p * rows : (p + 1) * rows]

    def rs_copy(d):
        to = other(d)
        return remote(rs_out.at[to], rs_in.at[d], rs_send.at[d], rs_recv.at[d], patch=to)

    peers(n, lambda d: rs_copy(d).start())
    peers(n, lambda d: rs_copy(d).wait_recv())
    total = rs_out[me]
    for d in range(1, n):
        total = total + rs_in[d]
    z_buf[mz] = total

    def z_copy(d):
        part = z_buf.at[mz]
        return remote(part, part, z_send.at[d], z_recv.at[d], head=other_z(d))

    peers(nz, lambda d: z_copy(d).start())
    peers(nz, lambda d: z_copy(d).wait_recv())
    total = z_buf[0]
    for d in range(1, nz):
        total = total + z_buf[d]
    ag[me] = total

    def ag_copy(d):
        part = ag.at[me]
        return remote(part, part, ag_send.at[d], ag_recv.at[d], patch=other(d))

    peers(n, lambda d: ag_copy(d).start())
    peers(n, lambda d: ag_copy(d).wait_recv())
    parts = []
    for p in range(n):
        part = jnp.zeros((rows, tok), F32)
        for s in range(REFRESH):
            part = jnp.where(is_mine[s], ag[p, s], part)
        parts.append(part)
    velocity = jnp.concatenate(parts, axis=0) + hid_t[...]
    wide = [
        jnp.concatenate([velocity[a * 32 : a * 32 + 16], velocity[a * 32 + 16 : a * 32 + 32]], axis=1)
        for a in range(2)
    ]
    wide = jnp.concatenate(wide, axis=0)
    one = wide.astype(BF16)
    left = wide - one.astype(F32)
    two = left.astype(BF16)
    three = (left - two.astype(F32)).astype(BF16)
    pieces = jnp.dot(
        jnp.concatenate([one, two, three], axis=0), spread[...], preferred_element_type=F32
    )
    field = pieces[:32] + pieces[32:64] + pieces[64:]
    for a in range(2):
        fresh_row = field[a * LAT_CH : (a + 1) * LAT_CH]
        row = jnp.where(mine, fresh_row, cache[a].astype(F32))
        latent = noisy[a].astype(F32) - noise[0] * row
        dec[a] = (latent / 0.3611 + 0.1159).astype(BF16)

    after, prior = lax.rem(me + 1, n), lax.rem(me + n - 1, n)
    edges = [
        remote(dec.at[1], halo.at[0], halo_send.at[0], halo_recv.at[0], patch=after),
        remote(dec.at[0], halo.at[1], halo_send.at[1], halo_recv.at[1], patch=prior),
    ]
    for copy in edges:
        copy.start()
    for copy in edges:
        copy.wait_recv()
    lines = [
        jnp.where(me > 0, halo[0].astype(F32), 0.0),
        dec[0].astype(F32),
        dec[1].astype(F32),
        jnp.where(me < n - 1, halo[1].astype(F32), 0.0),
    ]
    width = dec.shape[2]
    column = iota((LAT_CH, width), 1)
    shifted = []
    for line in lines:
        before_it = jnp.where(column == 0, 0.0, pltpu.roll(line, 1, 1))
        after_it = jnp.where(column == width - 1, 0.0, pltpu.roll(line, width - 1, 1))
        shifted.append([x.astype(BF16) for x in (before_it, line, after_it)])
    conv_col = to_column(conv_bias[...])
    for a in range(2):
        stencil = jnp.concatenate([shifted[a + u][v] for u in range(3) for v in range(3)], axis=0)
        result = lax.dot_general(conv_t[...], stencil, TN, preferred_element_type=F32)
        out[a] = (result + conv_col).astype(BF16)

    sent()
    for h in range(heads):
        peers(n, lambda d: st_copy(h, d).wait_send())
    peers(n, lambda d: rs_copy(d).wait_send())
    peers(nz, lambda d: z_copy(d).wait_send())
    peers(n, lambda d: ag_copy(d).wait_send())
    for copy in edges:
        copy.wait_send()


def on_device(
    n,
    nz,
    fresh_qkv,
    kv_cache,
    hidden,
    refresh,
    out_weight,
    final_weight,
    final_bias,
    gate_scale,
    noise_level,
    noisy_latent,
    velocity_cache,
    conv_weight,
    conv_bias,
):
    tok, _, local = fresh_qkv.shape
    heads = local // HEAD_DIM
    depth, vec = final_weight.shape
    rows = vec // n
    width = noisy_latent.shape[2]
    channels = conv_weight.shape[0]
    vmem, smem, anyw = (pl.BlockSpec(memory_space=m) for m in (pltpu.VMEM, pltpu.SMEM, pl.ANY))
    dma = pltpu.SemaphoreType.DMA
    kinds = 8 if n == 8 else n
    scratch = (
        [pltpu.VMEM((n, tok, HEAD_DIM), BF16)] * q_slots(n, heads)
        + [pltpu.VMEM((n, 2 * REFRESH, tok), F32)] * heads
        + [
            pltpu.VMEM((2, tok, local), BF16),
            pltpu.VMEM((tok, depth), BF16),
            pltpu.VMEM((local, depth), BF16),
            pltpu.VMEM((tok, local), BF16),
            pltpu.VMEM((heads, HEAD_DIM, tok), BF16),
            pltpu.VMEM((2 * vec, local), BF16),
            pltpu.VMEM((heads, REFRESH, vec, tok), F32),
            pltpu.VMEM((2 * tok, 2 * tok), BF16),
            pltpu.VMEM((vec, tok), F32),
            pltpu.VMEM((n, REFRESH, rows, tok), F32),
            pltpu.VMEM((n, REFRESH, rows, tok), F32),
            pltpu.VMEM((nz, REFRESH, rows, tok), F32),
            pltpu.VMEM((n, REFRESH, rows, tok), F32),
            pltpu.VMEM((2, LAT_CH, width), BF16),
            pltpu.VMEM((2, LAT_CH, width), BF16),
            dma((4,)),
            dma((heads,)),
            dma((heads, kinds)),
            dma((heads, kinds)),
            dma((heads, n)),
            dma((heads, n)),
            dma((n,)),
            dma((n,)),
            dma((nz,)),
            dma((nz,)),
            dma((n,)),
            dma((n,)),
            dma((2,)),
            dma((2,)),
            pltpu.SemaphoreType.REGULAR((heads,)),
        ]
    )
    return pl.pallas_call(
        functools.partial(kernel, n, nz, heads, tok),
        out_shape=jax.ShapeDtypeStruct((2, channels, width), BF16),
        in_specs=[smem, smem, anyw, vmem, anyw, anyw] + [vmem] * 7,
        out_specs=vmem,
        scratch_shapes=scratch,
        compiler_params=pltpu.CompilerParams(
            collective_id=0, has_side_effects=True, vmem_limit_bytes=58 * 1024 * 1024
        ),
    )(
        refresh,
        noise_level,
        jnp.transpose(fresh_qkv, (1, 0, 2)),
        kv_cache.reshape(2 * tok, local),
        hidden,
        out_weight,
        final_weight.T,
        final_bias[None, :],
        gate_scale[None, :],
        noisy_latent,
        velocity_cache,
        jnp.transpose(conv_weight, (1, 2, 3, 0)).reshape(-1, channels),
        conv_bias[None, :],
    )


def solution(mesh):
    return jax.shard_map(
        functools.partial(on_device, mesh.shape["patch"], mesh.shape["head"]),
        mesh=mesh,
        in_specs=(
            P("patch", None, "head"),
            P("patch", None, "head"),
            P("patch", None),
            P(),
            P("head", None),
            P(),
            P(),
            P(),
            P(),
            P("patch", None, None),
            P("patch", None, None),
            P("head", None, None, None),
            P("head"),
        ),
        out_specs=P("patch", "head", None),
        check_vma=False,
    )
```

time: 587 us -> 90 us (0.15); the launches traced: 579 us -> 89.8 us
  local copies, waits for them, and re-layouts: 257 us -> 6.55 us
  waiting for transfers between devices: 191 us -> 0 us
  Pallas kernels: 0 us -> 82.6 us
  matrix products: 52.1 us -> 0 us
  other arithmetic: 35.4 us -> 0 us
  blocking collectives: 23.7 us -> 0 us
  between operations: 17.1 us -> 0.66 us
    dynamic_update_slice x16 -> x0, local copies, waits for them, and re-layouts: 143 us -> none  [the longest x8 143 us: on_device(): numerator, denominator = lax.map(block_sums, (all_scores, maxima))]
    reduce_scatter x2 -> x0, waiting for transfers between devices: 89.4 us -> none  [the longest x1 65.2 us: on_device(): lax.psum_scatter(operand, 'patch', scatter_dimension=0, tiled=True)]
    pallas_call x0 -> x1, Pallas kernels: none -> 82.6 us  [on_device(): pl.pallas_call(functools.partial(kernel, n, nz, heads, tok), out_shape=ja...]
    all_gather x1 -> x0, waiting for transfers between devices: 54.5 us -> none  [on_device(): lax.all_gather(velocity_part, ('patch', 'head'), axis=0, tiled=True)]
    dynamic_slice x8 -> x0, local copies, waits for them, and re-layouts: 54 us -> none  [on_device(): numerator, denominator = lax.map(block_sums, (all_scores, maxima))]
    dot_general x12 -> x0, matrix products: 52.1 us -> none  [the longest x4 21.5 us: block_sums(): jnp.einsum('hqk,khd->qhd', exp_scores.astype(jnp.bfloat16), value_heads,...]
    psum x1 -> x0, waiting for transfers between devices: 44.5 us -> none  [broadcast(): return lax.psum(block, axis)]
    pmax x1 -> x0, blocking collectives: 23.7 us -> none  [on_device(): maxima = lax.pmax(maxima, 'patch')]
  transfers between devices with their start and end apart: 6 -> 0, of which waited for: 5 -> 0; matrix products, arithmetic and copies ran while one was open for 6% -> 0% of each run, Pallas kernels for 0% -> 0%
where the time goes in v1:
time: 90 us; the launch traced here: 89.8 us
  Pallas kernels  82.6 us (92%)
  local copies, waits for them, and re-layouts  6.55 us (7%)
    pallas_call x1, Pallas kernels, on_device(): pl.pallas_call(functools.partial(kernel, n, nz, heads, tok), out_shape=ja...  82.6 us
    reshape x1, local copies, waits for them, and re-layouts, on_device(): kv_cache.reshape(2 * tok, local)  4.68 us
    unnamed x1, local copies, waits for them, and re-layouts  1.87 us

profile of v1, /device:TPU:0, one launch (start us, length us, event | category | flops | bytes accessed | tf_op | source)
XLA Modules:
  0.0 89.8 jit_solution(15948670683608713482)
XLA Ops:
  0.7 4.7 %reshape.6.kv = bf16[1024,768]{1,0:T(8,128)(2,1)} reshape(bf16[512,2,768]{2,1,0:T(2,128)(2,1)} %param.14) | data formatting | bytes 3145728 | tf_op jit(solution)/shard_map/reshape | solution.py:497
  5.3 82.6 %shard_map.127 = bf16[2,128,1024]{2,1,0:T(8,128)(2,1)} custom-call(s32[4]{0:T(128)} %refresh.1, f32[1]{0:T(128)S(6)} %copy.15.noise, bf16[3,512,768]{2,1,0:T(8,128)(2,1)} %bitcast.8, bf16[1024,768]{1,0:T(8,128)(2,1)} %reshape.6.kv, bf16[512,3072]{1,0:T(8,128)(2,1)} %hidden.1, bf16[768,3072]{1,0:T(8,128)(2,1)} %out_weight.1, bf16[64,3072]{1,0:T(8,128)(2,1)} %bitcast.9, ...), custom_call_target="tpu_custom_call" | custom-call | tf_op jit(solution)/shard_map/pallas_call | solution.py:484
  87.9 1.9 %copy.16 = bf16[2,128,1024]{2,1,0:T(8,128)(2,1)} copy(bf16[2,128,1024]{2,1,0:T(8,128)(2,1)} %shard_map.127) | data formatting | bytes 1048576

commit v2 on v1

--- a/solution.py
+++ b/solution.py
@@ -69,7 +69,10 @@
         hid_t,
         rs_out,
         rs_in,
-        z_buf,
+        z_out,
+        z_in,
+        z_all,
+        ag_out,
         ag,
         dec,
         halo,
@@ -83,6 +86,8 @@
         rs_recv,
         z_send,
         z_recv,
+        zg_send,
+        zg_recv,
         ag_send,
         ag_recv,
         halo_send,
@@ -251,7 +256,7 @@
     loads[1].wait()
     for g in range(tok // group):
         at = pl.ds(g * group, group)
-        mixed = jnp.dot(unmix, kv[pl.ds(2 * g * group, 2 * group), :], preferred_element_type=F32)
+        mixed = jnp.dot(unmix, kv[pl.ds(g * group, group)].reshape(2 * group, -1), preferred_element_type=F32)
         mixed = mixed.astype(BF16)
         keys[at, :] = jnp.where(mine, fresh_kv[0, at, :], mixed[:group])
         picked = jnp.where(mine, fresh_kv[1, at, :], mixed[group:])
@@ -295,20 +300,30 @@
         before(h)
         cols = slice(h * HEAD_DIM, (h + 1) * HEAD_DIM)
 
-        @pl.loop(0, REFRESH)
-        def _(s):
-            query = q_all[h][refresh[s]]
-            scores = lax.dot_general(keys[:, cols], query, NT, preferred_element_type=F32)
-            top = jnp.max(scores, axis=0, keepdims=True)
-            weights = jnp.exp2((scores - top) * SCALE2)
-            stats[h][me, pl.ds(s, 1), :] = top
-            stats[h][me, pl.ds(s + REFRESH, 1), :] = jnp.sum(weights, axis=0, keepdims=True)
-            num = jnp.dot(values_t[h], weights.astype(BF16), preferred_element_type=F32)
-            num_hi = num.astype(BF16)
-            num_lo = (num - num_hi.astype(F32)).astype(BF16)
-            both = jnp.dot(w2[:, cols], num_hi, preferred_element_type=F32)
-            rest = jnp.dot(w2[:vec, cols], num_lo, preferred_element_type=F32)
-            u_buf[h, s] = both[:vec] + both[vec:] + rest
+        @pl.loop(0, REFRESH, step=2)
+        def _(base):
+            pair = (base, base + 1)
+            scores = [
+                lax.dot_general(
+                    keys[:, cols], q_all[h][refresh[s]], NT, preferred_element_type=F32
+                )
+                for s in pair
+            ]
+            nums = []
+            for s, score in zip(pair, scores):
+                top = jnp.max(score, axis=0, keepdims=True)
+                weights = jnp.exp2((score - top) * SCALE2)
+                stats[h][me, pl.ds(s, 1), :] = top
+                stats[h][me, pl.ds(s + REFRESH, 1), :] = jnp.sum(weights, axis=0, keepdims=True)
+                nums.append(
+                    jnp.dot(values_t[h], weights.astype(BF16), preferred_element_type=F32)
+                )
+            for s, num in zip(pair, nums):
+                num_hi = num.astype(BF16)
+                num_lo = (num - num_hi.astype(F32)).astype(BF16)
+                both = jnp.dot(w2[:, cols], num_hi, preferred_element_type=F32)
+                rest = jnp.dot(w2[:vec, cols], num_lo, preferred_element_type=F32)
+                u_buf[h, s] = both[:vec] + both[vec:] + rest
 
         peers(n, lambda d: st_copy(h, d).start())
         refill(h)
@@ -336,31 +351,39 @@
     total = rs_out[me]
     for d in range(1, n):
         total = total + rs_in[d]
-    z_buf[mz] = total
+    z_out[...] = total
 
     def z_copy(d):
-        part = z_buf.at[mz]
-        return remote(part, part, z_send.at[d], z_recv.at[d], head=other_z(d))
+        to = other_z(d)
+        return remote(z_out.at[to], z_in.at[d], z_send.at[d], z_recv.at[d], head=to)
 
     peers(nz, lambda d: z_copy(d).start())
     peers(nz, lambda d: z_copy(d).wait_recv())
-    total = z_buf[0]
+    total = z_out[mz]
     for d in range(1, nz):
-        total = total + z_buf[d]
-    ag[me] = total
+        total = total + z_in[d]
+    z_all[mz] = total
+
+    def zg_copy(d):
+        part = z_all.at[mz]
+        return remote(part, part, zg_send.at[d], zg_recv.at[d], head=other_z(d))
+
+    peers(nz, lambda d: zg_copy(d).start())
+    peers(nz, lambda d: zg_copy(d).wait_recv())
+    for p in range(n):
+        part = z_all[0]
+        for s in range(1, REFRESH):
+            part = jnp.where(refresh[s] == p, z_all[s], part)
+        ag_out[p] = part
 
     def ag_copy(d):
-        part = ag.at[me]
-        return remote(part, part, ag_send.at[d], ag_recv.at[d], patch=other(d))
+        to = other(d)
+        return remote(ag_out.at[to], ag.at[me], ag_send.at[d], ag_recv.at[d], patch=to)
 
     peers(n, lambda d: ag_copy(d).start())
+    ag[me] = ag_out[me]
     peers(n, lambda d: ag_copy(d).wait_recv())
-    parts = []
-    for p in range(n):
-        part = jnp.zeros((rows, tok), F32)
-        for s in range(REFRESH):
-            part = jnp.where(is_mine[s], ag[p, s], part)
-        parts.append(part)
+    parts = [ag[p] for p in range(n)]
     velocity = jnp.concatenate(parts, axis=0) + hid_t[...]
     wide = [
         jnp.concatenate([velocity[a * 32 : a * 32 + 16], velocity[a * 32 + 16 : a * 32 + 32]], axis=1)
@@ -414,6 +437,7 @@
         peers(n, lambda d: st_copy(h, d).wait_send())
     peers(n, lambda d: rs_copy(d).wait_send())
     peers(nz, lambda d: z_copy(d).wait_send())
+    peers(nz, lambda d: zg_copy(d).wait_send())
     peers(n, lambda d: ag_copy(d).wait_send())
     for copy in edges:
         copy.wait_send()
@@ -440,6 +464,7 @@
     heads = local // HEAD_DIM
     depth, vec = final_weight.shape
     rows = vec // n
+    assert nz == REFRESH
     width = noisy_latent.shape[2]
     channels = conv_weight.shape[0]
     vmem, smem, anyw = (pl.BlockSpec(memory_space=m) for m in (pltpu.VMEM, pltpu.SMEM, pl.ANY))
@@ -460,8 +485,11 @@
             pltpu.VMEM((vec, tok), F32),
             pltpu.VMEM((n, REFRESH, rows, tok), F32),
             pltpu.VMEM((n, REFRESH, rows, tok), F32),
-            pltpu.VMEM((nz, REFRESH, rows, tok), F32),
-            pltpu.VMEM((n, REFRESH, rows, tok), F32),
+            pltpu.VMEM((nz, rows, tok), F32),
+            pltpu.VMEM((nz, rows, tok), F32),
+            pltpu.VMEM((nz, rows, tok), F32),
+            pltpu.VMEM((n, rows, tok), F32),
+            pltpu.VMEM((n, rows, tok), F32),
             pltpu.VMEM((2, LAT_CH, width), BF16),
             pltpu.VMEM((2, LAT_CH, width), BF16),
             dma((4,)),
@@ -472,6 +500,8 @@
             dma((heads, n)),
             dma((n,)),
             dma((n,)),
+            dma((nz,)),
+            dma((nz,)),
             dma((nz,)),
             dma((nz,)),
             dma((n,)),
@@ -494,7 +524,7 @@
         refresh,
         noise_level,
         jnp.transpose(fresh_qkv, (1, 0, 2)),
-        kv_cache.reshape(2 * tok, local),
+        kv_cache,
         hidden,
         out_weight,
         final_weight.T,

time: 90 us -> 78.1 us (0.87)
  Pallas kernels: 82.6 us -> 75.4 us
  local copies, waits for them, and re-layouts: 6.55 us -> 1.87 us
    pallas_call x1, Pallas kernels: 82.6 us -> 75.4 us  [on_device(): pl.pallas_call(functools.partial(kernel, n, nz, heads, tok), out_shape=ja...]
    reshape x1 -> x0, local copies, waits for them, and re-layouts: 4.68 us -> none  [on_device(): kv_cache.reshape(2 * tok, local)]
where the time goes in v2:
time: 78.1 us; the launch traced here: 77.9 us
  Pallas kernels  75.4 us (97%)
  local copies, waits for them, and re-layouts  1.87 us (2%)
    pallas_call x1, Pallas kernels, on_device(): pl.pallas_call(functools.partial(kernel, n, nz, heads, tok), out_shape=ja...  75.4 us
    unnamed x1, local copies, waits for them, and re-layouts  1.87 us

profile of v2, /device:TPU:0, one launch (start us, length us, event | category | flops | bytes accessed | tf_op | source)
XLA Modules:
  0.0 77.9 jit_solution(3700548763989891587)
XLA Ops:
  0.7 75.4 %shard_map.127 = bf16[2,128,1024]{2,1,0:T(8,128)(2,1)} custom-call(s32[4]{0:T(128)} %refresh.1, f32[1]{0:T(128)S(6)} %copy.15.noise, bf16[3,512,768]{2,1,0:T(8,128)(2,1)} %bitcast.8, bf16[512,2,768]{2,1,0:T(2,128)(2,1)} %kv.1, bf16[512,3072]{1,0:T(8,128)(2,1)} %hidden.1, bf16[768,3072]{1,0:T(8,128)(2,1)} %out_weight.1, bf16[64,3072]{1,0:T(8,128)(2,1)} %bitcast.9, ...), custom_call_target="tpu_custom_call" | custom-call | tf_op jit(solution)/shard_map/pallas_call | solution.py:514
  76.0 1.9 %copy.16 = bf16[2,128,1024]{2,1,0:T(8,128)(2,1)} copy(bf16[2,128,1024]{2,1,0:T(8,128)(2,1)} %shard_map.127) | data formatting | bytes 1048576

commit v3 on v2

--- a/solution.py
+++ b/solution.py
@@ -57,6 +57,7 @@
     slots = q_slots(n, heads)
     q_all = [scratch[h % slots] for h in range(heads)]
     stats = scratch[slots : slots + heads]
+    chips = scratch[slots + heads : slots + 2 * heads]
     (
         fresh_kv,
         hidden_v,
@@ -93,7 +94,7 @@
         halo_send,
         halo_recv,
         free_sem,
-    ) = scratch[slots + heads :]
+    ) = scratch[slots + 2 * heads :]
     me = lax.axis_index("patch")
     mz = lax.axis_index("head")
     vec = final_t.shape[0]
@@ -142,6 +143,10 @@
         barrier, inc=1, device_id={"head": other_z(d)}, device_id_type=MESH))
     pl.semaphore_wait(barrier, n - 1 + nz - 1)
 
+    def st_copy(h, d):
+        part = stats[h].at[me]
+        return remote(part, part, st_send.at[h, d], st_recv.at[h, d], patch=other(d))
+
     if n == 8:
         near = me + 1 - 2 * lax.rem(me, 2)
         side = me + 2 - 4 * lax.rem(me // 2, 2)
@@ -189,22 +194,78 @@
             start(third(h))
 
         def before(h):
-            if h + 2 < heads:
-                start(first(h + 2))
-            if h + 1 < heads:
-                relay(h + 1)
-            relay_last(h)
             arrive(h, 2, q_all[h].at[near])
             arrive(h, 5, q_all[h].at[near_of(side)])
             arrive(h, 6, q_all[h].at[near_of(over)])
             arrive(h, 7, q_all[h].at[near_of(diag)])
 
+        def between(h):
+            if h + 1 < heads:
+                relay_last(h + 1)
+            if h + 2 < heads:
+                relay(h + 2)
+            if h + 3 < heads:
+                start(first(h + 3))
+            if h >= 1:
+                chip_stats(h - 1)
+
+        def chip_copies(h):
+            part = chips[h].at[me // 2]
+            return [
+                remote(part, part, st_send.at[h, k], st_recv.at[h, k], patch=to)
+                for k, to in ((1, side), (2, over), (3, diag))
+            ]
+
+        def chip_stats(h):
+            near_copy(h).wait_recv()
+            both = (stats[h][me], stats[h][near])
+            tops = [x[:REFRESH] for x in both]
+            top = jnp.maximum(*tops)
+            den = sum(x[REFRESH:] * jnp.exp2((x[:REFRESH] - top) * SCALE2) for x in both)
+            chips[h][me // 2, :REFRESH] = top
+            chips[h][me // 2, REFRESH:] = den
+            start(chip_copies(h))
+
+        def near_copy(h):
+            part = stats[h].at[me]
+            return remote(part, part, st_send.at[h, 0], st_recv.at[h, 0], patch=near)
+
+        def publish(h):
+            if h < heads - 1:
+                near_copy(h).start()
+            else:
+                peers(n, lambda d: st_copy(h, d).start())
+
+        def collect(h):
+            if h < heads - 1:
+                for copy in chip_copies(h):
+                    copy.wait_recv()
+                return chips[h][...]
+            peers(n, lambda d: st_copy(h, d).wait_recv())
+            return stats[h][...]
+
+        def published(h):
+            if h < heads - 1:
+                near_copy(h).wait_send()
+                for copy in chip_copies(h):
+                    copy.wait_send()
+            else:
+                peers(n, lambda d: st_copy(h, d).wait_send())
+
         def prologue():
-            for h in range(min(2, heads)):
-                start(first(h))
-
-        def middle():
-            relay(0)
+            start(first(0))
+
+        def middle(part):
+            if part == 0:
+                relay(0)
+                if heads > 1:
+                    start(first(1))
+            else:
+                relay_last(0)
+                if heads > 1:
+                    relay(1)
+                if heads > 2:
+                    start(first(2))
 
         def refill(h):
             pass
@@ -234,8 +295,21 @@
                 own_copies[later].start()
                 peers(n, lambda d: direct(later, d).start())
 
-        def middle():
+        def middle(part):
             pass
+
+        def between(h):
+            pass
+
+        def publish(h):
+            peers(n, lambda d: st_copy(h, d).start())
+
+        def collect(h):
+            peers(n, lambda d: st_copy(h, d).wait_recv())
+            return stats[h][...]
+
+        def published(h):
+            peers(n, lambda d: st_copy(h, d).wait_send())
 
         def before(h):
             peers(n, lambda d: direct(h, d).wait_recv())
@@ -265,7 +339,7 @@
             values_t[h, :, at] = lax.dot_general(
                 eye, picked[:, cols], NT, preferred_element_type=F32
             ).astype(BF16)
-    middle()
+    middle(0)
 
     k_of = iota((vec, vec), 1)
     r_of = iota((vec, vec), 0)
@@ -283,6 +357,7 @@
     w2_hi = w2_f.astype(BF16)
     w2[:vec, :] = w2_hi
     w2[vec:, :] = (w2_f - w2_hi.astype(F32)).astype(BF16)
+    middle(1)
     loads[3].wait()
     bias_col = jnp.sum(jnp.where(order, bias[...], 0.0), axis=1, keepdims=True)
     hid_t[...] = bias_col + lax.dot_general(
@@ -290,10 +365,6 @@
     )
     rr, cc = iota(spread.shape, 0), iota(spread.shape, 1)
     spread[...] = (cc == jnp.where(rr < tok, 2 * rr, 2 * (rr - tok) + 1)).astype(BF16)
-
-    def st_copy(h, d):
-        part = stats[h].at[me]
-        return remote(part, part, st_send.at[h, d], st_recv.at[h, d], patch=other(d))
 
     for h in range(heads):
         own_copies[h].wait()
@@ -325,13 +396,14 @@
                 rest = jnp.dot(w2[:vec, cols], num_lo, preferred_element_type=F32)
                 u_buf[h, s] = both[:vec] + both[vec:] + rest
 
-        peers(n, lambda d: st_copy(h, d).start())
+            pl.when(base == 0)(functools.partial(between, h))
+
+        publish(h)
         refill(h)
 
     sums = [jnp.zeros((vec, tok), F32) for _ in range(REFRESH)]
     for h in range(heads):
-        peers(n, lambda d: st_copy(h, d).wait_recv())
-        every = stats[h][...]
+        every = collect(h)
         tops, dens = every[:, :REFRESH], every[:, REFRESH:]
         top = jnp.max(tops, axis=0)
         den = jnp.sum(dens * jnp.exp2((tops - top[None]) * SCALE2), axis=0)
@@ -434,7 +506,7 @@
 
     sent()
     for h in range(heads):
-        peers(n, lambda d: st_copy(h, d).wait_send())
+        published(h)
     peers(n, lambda d: rs_copy(d).wait_send())
     peers(nz, lambda d: z_copy(d).wait_send())
     peers(nz, lambda d: zg_copy(d).wait_send())
@@ -473,6 +545,7 @@
     scratch = (
         [pltpu.VMEM((n, tok, HEAD_DIM), BF16)] * q_slots(n, heads)
         + [pltpu.VMEM((n, 2 * REFRESH, tok), F32)] * heads
+        + [pltpu.VMEM((max(n // 2, 1), 2 * REFRESH, tok), F32)] * heads
         + [
             pltpu.VMEM((2, tok, local), BF16),
             pltpu.VMEM((tok, depth), BF16),

time: 78.1 us -> 80.4 us (1.029)
  Pallas kernels: 75.4 us -> 77.7 us
    pallas_call x1, Pallas kernels: 75.4 us -> 77.7 us  [on_device(): pl.pallas_call(functools.partial(kernel, n, nz, heads, tok), out_shape=ja...]
where the time goes in v3:
time: 80.4 us; the launch traced here: 80.2 us
  Pallas kernels  77.7 us (97%)
  local copies, waits for them, and re-layouts  1.87 us (2%)
    pallas_call x1, Pallas kernels, on_device(): pl.pallas_call(functools.partial(kernel, n, nz, heads, tok), out_shape=ja...  77.7 us
    unnamed x1, local copies, waits for them, and re-layouts  1.87 us

profile of v3, /device:TPU:0, one launch (start us, length us, event | category | flops | bytes accessed | tf_op | source)
XLA Modules:
  0.0 80.2 jit_solution(8724488567224613936)
XLA Ops:
  0.7 77.7 %shard_map.127 = bf16[2,128,1024]{2,1,0:T(8,128)(2,1)} custom-call(s32[4]{0:T(128)} %refresh.1, f32[1]{0:T(128)S(6)} %copy.15.noise, bf16[3,512,768]{2,1,0:T(8,128)(2,1)} %bitcast.8, bf16[512,2,768]{2,1,0:T(2,128)(2,1)} %kv.1, bf16[512,3072]{1,0:T(8,128)(2,1)} %hidden.1, bf16[768,3072]{1,0:T(8,128)(2,1)} %out_weight.1, bf16[64,3072]{1,0:T(8,128)(2,1)} %bitcast.9, ...), custom_call_target="tpu_custom_call" | custom-call | tf_op jit(solution)/shard_map/pallas_call | solution.py:587
  78.3 1.9 %copy.16 = bf16[2,128,1024]{2,1,0:T(8,128)(2,1)} copy(bf16[2,128,1024]{2,1,0:T(8,128)(2,1)} %shard_map.127) | data formatting | bytes 1048576

commit v4 on v3

--- a/solution.py
+++ b/solution.py
@@ -12,7 +12,7 @@
 LAT_CH = 16
 REFRESH = 4
 MESH = pl.DeviceIdType.MESH
-SCALE2 = math.log2(math.e) / math.sqrt(HEAD_DIM)
+SCALE = 1.0 / math.sqrt(HEAD_DIM)
 NT = (((1,), (1,)), ((), ()))
 TN = (((0,), (0,)), ((), ()))
 F32 = jnp.float32
@@ -68,6 +68,7 @@
         u_buf,
         spread,
         hid_t,
+        rows_t,
         rs_out,
         rs_in,
         z_out,
@@ -204,8 +205,8 @@
                 relay_last(h + 1)
             if h + 2 < heads:
                 relay(h + 2)
-            if h + 3 < heads:
-                start(first(h + 3))
+            if h + 5 < heads:
+                start(first(h + 5))
             if h >= 1:
                 chip_stats(h - 1)
 
@@ -221,7 +222,7 @@
             both = (stats[h][me], stats[h][near])
             tops = [x[:REFRESH] for x in both]
             top = jnp.maximum(*tops)
-            den = sum(x[REFRESH:] * jnp.exp2((x[:REFRESH] - top) * SCALE2) for x in both)
+            den = sum(x[REFRESH:] * jnp.exp((x[:REFRESH] - top) * SCALE) for x in both)
             chips[h][me // 2, :REFRESH] = top
             chips[h][me // 2, REFRESH:] = den
             start(chip_copies(h))
@@ -253,19 +254,20 @@
                 peers(n, lambda d: st_copy(h, d).wait_send())
 
         def prologue():
-            start(first(0))
+            for h in range(min(3, heads)):
+                start(first(h))
 
         def middle(part):
             if part == 0:
                 relay(0)
-                if heads > 1:
-                    start(first(1))
+                if heads > 3:
+                    start(first(3))
             else:
                 relay_last(0)
                 if heads > 1:
                     relay(1)
-                if heads > 2:
-                    start(first(2))
+                if heads > 4:
+                    start(first(4))
 
         def refill(h):
             pass
@@ -346,6 +348,7 @@
     row_k = (r_of & (LAT_CH - 1)) * 4 + (r_of >> 5) * 2 + ((r_of >> 4) & 1)
     order = k_of == row_k
     final_rows = jnp.dot(order.astype(BF16), final_t[...], preferred_element_type=F32)
+    rows_t[...] = final_rows.astype(BF16)
     gated = final_rows * gate[...]
     gated_hi = gated.astype(BF16)
     gated_lo = (gated - gated_hi.astype(F32)).astype(BF16)
@@ -358,13 +361,6 @@
     w2[:vec, :] = w2_hi
     w2[vec:, :] = (w2_f - w2_hi.astype(F32)).astype(BF16)
     middle(1)
-    loads[3].wait()
-    bias_col = jnp.sum(jnp.where(order, bias[...], 0.0), axis=1, keepdims=True)
-    hid_t[...] = bias_col + lax.dot_general(
-        final_rows.astype(BF16), hidden_v[...], NT, preferred_element_type=F32
-    )
-    rr, cc = iota(spread.shape, 0), iota(spread.shape, 1)
-    spread[...] = (cc == jnp.where(rr < tok, 2 * rr, 2 * (rr - tok) + 1)).astype(BF16)
 
     for h in range(heads):
         own_copies[h].wait()
@@ -383,7 +379,7 @@
             nums = []
             for s, score in zip(pair, scores):
                 top = jnp.max(score, axis=0, keepdims=True)
-                weights = jnp.exp2((score - top) * SCALE2)
+                weights = jnp.exp((score - top) * SCALE)
                 stats[h][me, pl.ds(s, 1), :] = top
                 stats[h][me, pl.ds(s + REFRESH, 1), :] = jnp.sum(weights, axis=0, keepdims=True)
                 nums.append(
@@ -406,8 +402,8 @@
         every = collect(h)
         tops, dens = every[:, :REFRESH], every[:, REFRESH:]
         top = jnp.max(tops, axis=0)
-        den = jnp.sum(dens * jnp.exp2((tops - top[None]) * SCALE2), axis=0)
-        factor = jnp.exp2((stats[h][me][:REFRESH] - top) * SCALE2) / den
+        den = jnp.sum(dens * jnp.exp((tops - top[None]) * SCALE), axis=0)
+        factor = jnp.exp((stats[h][me][:REFRESH] - top) * SCALE) / den
         for s in range(REFRESH):
             sums[s] = sums[s] + u_buf[h, s] * factor[s : s + 1]
     for p in range(n):
@@ -419,6 +415,11 @@
         return remote(rs_out.at[to], rs_in.at[d], rs_send.at[d], rs_recv.at[d], patch=to)
 
     peers(n, lambda d: rs_copy(d).start())
+    loads[3].wait()
+    bias_col = jnp.sum(jnp.where(order, bias[...], 0.0), axis=1, keepdims=True)
+    hid_t[...] = bias_col + lax.dot_general(
+        rows_t[...], hidden_v[...], NT, preferred_element_type=F32
+    )
     peers(n, lambda d: rs_copy(d).wait_recv())
     total = rs_out[me]
     for d in range(1, n):
@@ -430,6 +431,8 @@
         return remote(z_out.at[to], z_in.at[d], z_send.at[d], z_recv.at[d], head=to)
 
     peers(nz, lambda d: z_copy(d).start())
+    rr, cc = iota(spread.shape, 0), iota(spread.shape, 1)
+    spread[...] = (cc == jnp.where(rr < tok, 2 * rr, 2 * (rr - tok) + 1)).astype(BF16)
     peers(nz, lambda d: z_copy(d).wait_recv())
     total = z_out[mz]
     for d in range(1, nz):
@@ -556,6 +559,7 @@
             pltpu.VMEM((heads, REFRESH, vec, tok), F32),
             pltpu.VMEM((2 * tok, 2 * tok), BF16),
             pltpu.VMEM((vec, tok), F32),
+            pltpu.VMEM((vec, depth), BF16),
             pltpu.VMEM((n, REFRESH, rows, tok), F32),
             pltpu.VMEM((n, REFRESH, rows, tok), F32),
             pltpu.VMEM((nz, rows, tok), F32),

time: 80.4 us -> 74.7 us (0.929)
  Pallas kernels: 77.7 us -> 71.9 us
    pallas_call x1, Pallas kernels: 77.7 us -> 71.9 us  [on_device(): pl.pallas_call(functools.partial(kernel, n, nz, heads, tok), out_shape=ja...]
where the time goes in v4:
time: 74.7 us; the launch traced here: 74.5 us
  Pallas kernels  71.9 us (96%)
  local copies, waits for them, and re-layouts  1.87 us (3%)
    pallas_call x1, Pallas kernels, on_device(): pl.pallas_call(functools.partial(kernel, n, nz, heads, tok), out_shape=ja...  71.9 us
    unnamed x1, local copies, waits for them, and re-layouts  1.87 us

profile of v4, /device:TPU:0, one launch (start us, length us, event | category | flops | bytes accessed | tf_op | source)
XLA Modules:
  0.0 74.5 jit_solution(292919126625462799)
XLA Ops:
  0.7 71.9 %shard_map.127 = bf16[2,128,1024]{2,1,0:T(8,128)(2,1)} custom-call(s32[4]{0:T(128)} %refresh.1, f32[1]{0:T(128)S(6)} %copy.15.noise, bf16[3,512,768]{2,1,0:T(8,128)(2,1)} %bitcast.8, bf16[512,2,768]{2,1,0:T(2,128)(2,1)} %kv.1, bf16[512,3072]{1,0:T(8,128)(2,1)} %hidden.1, bf16[768,3072]{1,0:T(8,128)(2,1)} %out_weight.1, bf16[64,3072]{1,0:T(8,128)(2,1)} %bitcast.9, ...), custom_call_target="tpu_custom_call" | custom-call | tf_op jit(solution)/shard_map/pallas_call | solution.py:591
  72.6 1.9 %copy.16 = bf16[2,128,1024]{2,1,0:T(8,128)(2,1)} copy(bf16[2,128,1024]{2,1,0:T(8,128)(2,1)} %shard_map.127) | data formatting | bytes 1048576

commit v5 on v4

--- a/solution.py
+++ b/solution.py
@@ -12,7 +12,7 @@
 LAT_CH = 16
 REFRESH = 4
 MESH = pl.DeviceIdType.MESH
-SCALE = 1.0 / math.sqrt(HEAD_DIM)
+SCALE = math.log2(math.e) / math.sqrt(HEAD_DIM)
 NT = (((1,), (1,)), ((), ()))
 TN = (((0,), (0,)), ((), ()))
 F32 = jnp.float32
@@ -69,6 +69,7 @@
         spread,
         hid_t,
         rows_t,
+        num_buf,
         rs_out,
         rs_in,
         z_out,
@@ -222,7 +223,7 @@
             both = (stats[h][me], stats[h][near])
             tops = [x[:REFRESH] for x in both]
             top = jnp.maximum(*tops)
-            den = sum(x[REFRESH:] * jnp.exp((x[:REFRESH] - top) * SCALE) for x in both)
+            den = sum(x[REFRESH:] * jnp.exp2((x[:REFRESH] - top) * SCALE) for x in both)
             chips[h][me // 2, :REFRESH] = top
             chips[h][me // 2, REFRESH:] = den
             start(chip_copies(h))
@@ -343,23 +344,6 @@
             ).astype(BF16)
     middle(0)
 
-    k_of = iota((vec, vec), 1)
-    r_of = iota((vec, vec), 0)
-    row_k = (r_of & (LAT_CH - 1)) * 4 + (r_of >> 5) * 2 + ((r_of >> 4) & 1)
-    order = k_of == row_k
-    final_rows = jnp.dot(order.astype(BF16), final_t[...], preferred_element_type=F32)
-    rows_t[...] = final_rows.astype(BF16)
-    gated = final_rows * gate[...]
-    gated_hi = gated.astype(BF16)
-    gated_lo = (gated - gated_hi.astype(F32)).astype(BF16)
-    loads[2].wait()
-    w2_f = lax.dot_general(
-        jnp.concatenate([gated_hi, gated_lo], axis=0), weight_v[...], NT, preferred_element_type=F32
-    )
-    w2_f = w2_f[:vec] + w2_f[vec:]
-    w2_hi = w2_f.astype(BF16)
-    w2[:vec, :] = w2_hi
-    w2[vec:, :] = (w2_f - w2_hi.astype(F32)).astype(BF16)
     middle(1)
 
     for h in range(heads):
@@ -379,36 +363,60 @@
             nums = []
             for s, score in zip(pair, scores):
                 top = jnp.max(score, axis=0, keepdims=True)
-                weights = jnp.exp((score - top) * SCALE)
+                weights = jnp.exp2((score - top) * SCALE)
                 stats[h][me, pl.ds(s, 1), :] = top
                 stats[h][me, pl.ds(s + REFRESH, 1), :] = jnp.sum(weights, axis=0, keepdims=True)
                 nums.append(
                     jnp.dot(values_t[h], weights.astype(BF16), preferred_element_type=F32)
                 )
             for s, num in zip(pair, nums):
-                num_hi = num.astype(BF16)
-                num_lo = (num - num_hi.astype(F32)).astype(BF16)
-                both = jnp.dot(w2[:, cols], num_hi, preferred_element_type=F32)
-                rest = jnp.dot(w2[:vec, cols], num_lo, preferred_element_type=F32)
-                u_buf[h, s] = both[:vec] + both[vec:] + rest
+                num_buf[s] = num
 
             pl.when(base == 0)(functools.partial(between, h))
 
         publish(h)
         refill(h)
+        if h == 0:
+            k_of = iota((vec, vec), 1)
+            r_of = iota((vec, vec), 0)
+            row_k = (r_of & (LAT_CH - 1)) * 4 + (r_of >> 5) * 2 + ((r_of >> 4) & 1)
+            order = k_of == row_k
+            final_rows = jnp.dot(order.astype(BF16), final_t[...], preferred_element_type=F32)
+            rows_t[...] = final_rows.astype(BF16)
+            gated = final_rows * gate[...]
+            gated_hi = gated.astype(BF16)
+            gated_lo = (gated - gated_hi.astype(F32)).astype(BF16)
+            loads[2].wait()
+            w2_f = lax.dot_general(
+                jnp.concatenate([gated_hi, gated_lo], axis=0), weight_v[...], NT, preferred_element_type=F32
+            )
+            w2_f = w2_f[:vec] + w2_f[vec:]
+            w2_hi = w2_f.astype(BF16)
+            w2[:vec, :] = w2_hi
+            w2[vec:, :] = (w2_f - w2_hi.astype(F32)).astype(BF16)
+
+        @pl.loop(0, REFRESH)
+        def _(s):
+            num = num_buf[s]
+            num_hi = num.astype(BF16)
+            num_lo = (num - num_hi.astype(F32)).astype(BF16)
+            both = jnp.dot(w2[:, cols], num_hi, preferred_element_type=F32)
+            rest = jnp.dot(w2[:vec, cols], num_lo, preferred_element_type=F32)
+            u_buf[h, s] = both[:vec] + both[vec:] + rest
 
     sums = [jnp.zeros((vec, tok), F32) for _ in range(REFRESH)]
     for h in range(heads):
         every = collect(h)
         tops, dens = every[:, :REFRESH], every[:, REFRESH:]
         top = jnp.max(tops, axis=0)
-        den = jnp.sum(dens * jnp.exp((tops - top[None]) * SCALE), axis=0)
-        factor = jnp.exp((stats[h][me][:REFRESH] - top) * SCALE) / den
+        den = jnp.sum(dens * jnp.exp2((tops - top[None]) * SCALE), axis=0)
+        factor = jnp.exp2((stats[h][me][:REFRESH] - top) * SCALE) / den
         for s in range(REFRESH):
             sums[s] = sums[s] + u_buf[h, s] * factor[s : s + 1]
     for p in range(n):
         for s in range(REFRESH):
-            rs_out[p, s] = sums[s][p * rows : (p + 1) * rows]
+            part = sums[s][p * rows : (p + 1) * rows]
+            rs_out[p, s * rows : (s + 1) * rows] = part.astype(rs_out.dtype)
 
     def rs_copy(d):
         to = other(d)
@@ -421,10 +429,11 @@
         rows_t[...], hidden_v[...], NT, preferred_element_type=F32
     )
     peers(n, lambda d: rs_copy(d).wait_recv())
-    total = rs_out[me]
+    total = rs_out[me].astype(F32)
     for d in range(1, n):
-        total = total + rs_in[d]
-    z_out[...] = total
+        total = total + rs_in[d].astype(F32)
+    for s in range(REFRESH):
+        z_out[s] = total[s * rows : (s + 1) * rows]
 
     def z_copy(d):
         to = other_z(d)
@@ -560,8 +569,9 @@
             pltpu.VMEM((2 * tok, 2 * tok), BF16),
             pltpu.VMEM((vec, tok), F32),
             pltpu.VMEM((vec, depth), BF16),
-            pltpu.VMEM((n, REFRESH, rows, tok), F32),
-            pltpu.VMEM((n, REFRESH, rows, tok), F32),
+            pltpu.VMEM((REFRESH, HEAD_DIM, tok), F32),
+            pltpu.VMEM((n, REFRESH * rows, tok), BF16 if rows % 8 == 0 else F32),
+            pltpu.VMEM((n, REFRESH * rows, tok), BF16 if rows % 8 == 0 else F32),
             pltpu.VMEM((nz, rows, tok), F32),
             pltpu.VMEM((nz, rows, tok), F32),
             pltpu.VMEM((nz, rows, tok), F32),

time: 74.7 us -> 71.8 us (0.961)
  Pallas kernels: 71.9 us -> 69.1 us
    pallas_call x1, Pallas kernels: 71.9 us -> 69.1 us  [on_device(): pl.pallas_call(functools.partial(kernel, n, nz, heads, tok), out_shape=ja...]
where the time goes in v5:
time: 71.8 us; the launch traced here: 71.6 us
  Pallas kernels  69.1 us (96%)
  local copies, waits for them, and re-layouts  1.87 us (3%)
    pallas_call x1, Pallas kernels, on_device(): pl.pallas_call(functools.partial(kernel, n, nz, heads, tok), out_shape=ja...  69.1 us
    unnamed x1, local copies, waits for them, and re-layouts  1.87 us

profile of v5, /device:TPU:0, one launch (start us, length us, event | category | flops | bytes accessed | tf_op | source)
XLA Modules:
  0.0 71.6 jit_solution(14000031332258716986)
XLA Ops:
  0.7 69.1 %shard_map.127 = bf16[2,128,1024]{2,1,0:T(8,128)(2,1)} custom-call(s32[4]{0:T(128)} %refresh.1, f32[1]{0:T(128)S(6)} %copy.15.noise, bf16[3,512,768]{2,1,0:T(8,128)(2,1)} %bitcast.8, bf16[512,2,768]{2,1,0:T(2,128)(2,1)} %kv.1, bf16[512,3072]{1,0:T(8,128)(2,1)} %hidden.1, bf16[768,3072]{1,0:T(8,128)(2,1)} %out_weight.1, bf16[64,3072]{1,0:T(8,128)(2,1)} %bitcast.9, ...), custom_call_target="tpu_custom_call" | custom-call | tf_op jit(solution)/shard_map/pallas_call | solution.py:601
  69.8 1.9 %copy.16 = bf16[2,128,1024]{2,1,0:T(8,128)(2,1)} copy(bf16[2,128,1024]{2,1,0:T(8,128)(2,1)} %shard_map.127) | data formatting | bytes 1048576

commit v6 on v5

--- a/solution.py
+++ b/solution.py
@@ -135,7 +135,7 @@
     own_copies = [
         pltpu.make_async_copy(own_q[h], q_all[h].at[me], own_sem.at[h]) for h in range(heads)
     ]
-    for copy in loads + own_copies[:slots]:
+    for copy in loads[:2] + own_copies[:slots]:
         copy.start()
 
     barrier = pltpu.get_barrier_semaphore()
@@ -322,6 +322,8 @@
                 peers(n, lambda d: direct(h, d).wait_send())
 
     prologue()
+    for copy in loads[2:]:
+        copy.start()
 
     is_mine = [refresh[s] == me for s in range(REFRESH)]
     mine = is_mine[0] | is_mine[1] | is_mine[2] | is_mine[3]

time: 71.8 us -> 71.8 us (level)
  no operation moved by 1% of the time
where the time goes in v6:
time: 71.8 us; the launch traced here: 71.6 us
  Pallas kernels  69.1 us (96%)
  local copies, waits for them, and re-layouts  1.87 us (3%)
    pallas_call x1, Pallas kernels, on_device(): pl.pallas_call(functools.partial(kernel, n, nz, heads, tok), out_shape=ja...  69.1 us
    unnamed x1, local copies, waits for them, and re-layouts  1.87 us

profile of v6, /device:TPU:0, one launch (start us, length us, event | category | flops | bytes accessed | tf_op | source)
XLA Modules:
  0.0 71.6 jit_solution(5297346752908050684)
XLA Ops:
  0.7 69.1 %shard_map.127 = bf16[2,128,1024]{2,1,0:T(8,128)(2,1)} custom-call(s32[4]{0:T(128)} %refresh.1, f32[1]{0:T(128)S(6)} %copy.15.noise, bf16[3,512,768]{2,1,0:T(8,128)(2,1)} %bitcast.8, bf16[512,2,768]{2,1,0:T(2,128)(2,1)} %kv.1, bf16[512,3072]{1,0:T(8,128)(2,1)} %hidden.1, bf16[768,3072]{1,0:T(8,128)(2,1)} %out_weight.1, bf16[64,3072]{1,0:T(8,128)(2,1)} %bitcast.9, ...), custom_call_target="tpu_custom_call" | custom-call | tf_op jit(solution)/shard_map/pallas_call | solution.py:603
  69.7 1.9 %copy.16 = bf16[2,128,1024]{2,1,0:T(8,128)(2,1)} copy(bf16[2,128,1024]{2,1,0:T(8,128)(2,1)} %shard_map.127) | data formatting | bytes 1048576
